TPU v7x, 512 devices: a whole 4x4x16 slice. The times are simulated.
512 devices in a mesh: scan: 128 (over z, x, core), bin: 4 (over y).
Axes of the slice: x: 4, y: 4, z: 16, core: 2. Of those that a mesh axis runs over, the one named last changes fastest.
Arguments:
- tile_blocks: bfloat16 [1024, 16, 256, 256], P('scan', 'bin'), may hold values from -0.25 to 0.25
- tile_pattern: int32 [2, 1024], P(None, 'scan'), may hold values from 0 to 255, as said below
- tile_count: int32 [128], P('scan'), may hold values from 1 to 8, as said below
- initial_map: float32 [16, 4, 65536], P('bin', None, 'scan')
- measured: float32 [16, 4, 16384], P('bin', None, 'scan')
- step_size: float32 [1], replicated, may hold values from 0.06 to 0.1
- penalty: float32 [65536], P('scan'), may hold values from 40 to 200
Outputs:
- source_map: float32 [16, 4, 65536], P('bin', None, 'scan')
Inputs may be any that keep to these rules, and one draw needn't show every extreme that they name: `tile_pattern`: row 0 names a sensor block of 64; row 1 of slot s names one of the 2 scan tiles (s // 8) * 2 to (s // 8) * 2 + 1. Only the first tile_count[d] slots of index d of scan are live; in every draw some indices have all 8 slots live.
All inputs are finite; a program needn't handle non-finite values.
Results may differ from a plain program's by a relative error of at most 0.00074.
Values may be sent and summed in bfloat16 or wider, within the bound.
A program may use at most 64 MiB of HBM per device.

v0:
```python
import jax
import jax.numpy as jnp
from jax import lax
from jax.sharding import PartitionSpec as P

ITERS = 2


def add_forward(partial_value, tile_set, block_rows, block_cols, points, first_slot, end_slot):
    tile_width = tile_set.shape[-1]

    def advance(slot_id, running):
        matrix = lax.dynamic_index_in_dim(tile_set, slot_id, 0, keepdims=False)
        source = lax.dynamic_slice_in_dim(points, block_cols[slot_id] * tile_width, tile_width, 2)
        contrib = jnp.einsum("fij,fsj->fsi", matrix, source, preferred_element_type=jnp.float32)
        start = block_rows[slot_id] * tile_width
        present = lax.dynamic_slice_in_dim(running, start, tile_width, 2)
        return lax.dynamic_update_slice_in_dim(running, present + contrib, start, 2)

    return lax.fori_loop(first_slot, end_slot, advance, partial_value)


def add_backward(gradient, tile_set, block_rows, block_cols, residual, first_slot, end_slot):
    tile_width = tile_set.shape[-1]

    def advance(slot_id, running):
        matrix = lax.dynamic_index_in_dim(tile_set, slot_id, 0, keepdims=False)
        source = lax.dynamic_slice_in_dim(residual, block_rows[slot_id] * tile_width, tile_width, 2)
        contrib = jnp.einsum("fij,fsi->fsj", matrix, source, preferred_element_type=jnp.float32)
        start = block_cols[slot_id] * tile_width
        present = lax.dynamic_slice_in_dim(running, start, tile_width, 2)
        return lax.dynamic_update_slice_in_dim(running, present + contrib, start, 2)

    return lax.fori_loop(first_slot, end_slot, advance, gradient)


def body(tile_blocks, tile_pattern, tile_count, initial_map, measured, step_size, penalty):
    tile_width = tile_blocks.shape[-1]
    per_device = initial_map.shape[2] // tile_width
    block_rows = tile_pattern[0]
    block_cols = tile_pattern[1] - lax.axis_index("scan") * per_device
    live_count = tile_count[0]
    bins_dev, snapshots, sensors_dev = measured.shape
    scan_count = lax.axis_size("scan")
    sensors = sensors_dev * scan_count
    measured_all = lax.all_gather(measured, "scan", axis=2, tiled=True)
    current = initial_map
    for iteration in range(ITERS):
        rounded_map = current.astype(jnp.bfloat16)
        partial_value = jnp.zeros((bins_dev, snapshots, sensors), jnp.float32)
        partial_value = add_forward(
            partial_value, tile_blocks, block_rows, block_cols, rounded_map, 0, live_count
        )
        totals = lax.psum(partial_value, "scan")
        residual = (totals - measured_all).astype(jnp.bfloat16)
        gradient = jnp.zeros_like(current)
        gradient = add_backward(
            gradient, tile_blocks, block_rows, block_cols, residual, 0, live_count
        )
        moved = current - step_size[0] * gradient
        energy = lax.psum(jnp.sum(moved * moved, axis=(0, 1)), "bin")
        current = moved * jnp.maximum(0.0, 1.0 - step_size[0] * penalty / jnp.sqrt(energy + 1e-06))
    return current


def solution(mesh):
    in_specs = (
        P("scan", "bin", None, None),
        P(None, "scan"),
        P("scan"),
        P("bin", None, "scan"),
        P("bin", None, "scan"),
        P(),
        P("scan"),
    )
    out_specs = P("bin", None, "scan")
    return jax.shard_map(body, mesh=mesh, in_specs=in_specs, out_specs=out_specs, check_vma=False)
```

profile of v0, /device:TPU:1, one launch (start us, length us, event | category | flops | bytes accessed | tf_op | source)
XLA Modules:
  0.0 987.4 jit_solution(17317380902763348420)
XLA Ops:
  6.5 0.8 convert_element_type.12
  7.3 0.8 slice_bitcast_fusion
  8.2 37.1 %while.40 = (s32[]{:T(128)}, f32[4,4,16384]{2,1,0:T(4,128)S(1)}, s32[]{:T(128)}, s32[8]{0:T(128)S(1)}, s32[8]{0:T(128)S(1)}, /*index=5*/bf16[4,4,512]{2,1,0:T(4,...) while((s32[]{:T(128)}, f32[4,4,16384]{2,1,0:T(4,128)S(1)}, ...), condition=%wide.region_1.2_spmd, body=%wide.region_0.1_spmd.sunk | while | flops 2101261 | bytes 565535 | solution.py:20
  10.2 0.7 dynamic_slice.112
  11.5 1.3 fusion.34
  16.0 1.3 fusion.34
  20.6 1.3 fusion.34
  25.1 1.3 fusion.34
  29.7 1.3 fusion.34
  33.0 0.7 dynamic_slice.112
  34.3 1.3 fusion.34
  38.8 1.3 fusion.34
  42.1 0.7 dynamic_slice.112
  43.4 1.3 fusion.34
  45.4 1.0 copy-done
  46.4 0.7 all-gather.2.cloned.1.call-update
  47.8 338.4 %all-reduce.3.cloned.1.call-done = f32[4,4,16384]{2,1,0:T(4,128)} async-done(((f32[4,4,16384]{2,1,0:T(4,128)}), f32[4,4,16384]{2,1,0:T(4,128)}) %all-reduce.3.cloned.1.call-update) | async-done | bytes 1048592 | tf_op jit(solution)/shard_map/psum | solution.py:54
  386.2 132.1 %all-gather.2.cloned.1.call-done = f32[4,4,16384]{2,1,0:T(4,128)} async-done(((f32[4,4,128]{2,1,0:T(4,128)}), f32[4,4,16384]{2,1,0:T(4,128)}) %all-gather.2.cloned.1.call-update) | async-done | bytes 1048592 | tf_op jit(solution)/shard_map/all_gather | solution.py:46
  518.3 1.8 subtract_convert_fusion.1
  520.2 36.7 %while.41 = (s32[]{:T(128)}, f32[4,4,512]{2,1,0:T(4,128)S(1)}, s32[]{:T(128)}, s32[8]{0:T(128)S(1)}, s32[8]{0:T(128)S(1)}, /*index=5*/bf16[4,4,16384]{2,1,0:T(4,...) while((s32[]{:T(128)}, f32[4,4,512]{2,1,0:T(4,128)S(1)}, ...), condition=%wide.region_4.5_spmd, body=%wide.region_3.4_spmd.sunk | while | flops 2101261 | bytes 565535 | solution.py:34
  523.5 1.2 fusion.37
  526.7 0.7 dynamic_slice.117
  528.0 1.2 fusion.37
  531.2 0.7 dynamic_slice.117
  532.5 1.2 fusion.37
  537.0 1.2 fusion.37
  541.5 1.2 fusion.37
  546.0 1.2 fusion.37
  550.5 1.2 fusion.37
  553.7 0.7 dynamic_slice.117
  555.0 1.2 fusion.37
  556.9 8.5 psum.29
  565.5 37.1 %while.42 = (s32[]{:T(128)}, f32[4,4,16384]{2,1,0:T(4,128)S(1)}, s32[]{:T(128)}, s32[8]{0:T(128)S(1)}, s32[8]{0:T(128)S(1)}, /*index=5*/bf16[4,4,512]{2,1,0:T(4,...) while((s32[]{:T(128)}, f32[4,4,16384]{2,1,0:T(4,128)S(1)}, ...), condition=%wide.region_8.9_spmd, body=%wide.region_7.8_spmd.sunk | while | flops 2101261 | bytes 565535 | solution.py:20
  567.5 0.7 dynamic_slice.122
  568.8 1.3 fusion.40
  572.1 0.7 dynamic_slice.122
  573.4 1.3 fusion.40
  576.6 0.7 dynamic_slice.122
  577.9 1.3 fusion.40
  582.5 1.3 fusion.40
  587.0 1.3 fusion.40
  590.3 0.7 dynamic_slice.122
  591.6 1.3 fusion.40
  594.9 0.7 dynamic_slice.122
  596.2 1.3 fusion.40
  599.4 0.7 dynamic_slice.122
  600.7 1.3 fusion.40
  602.7 1.0 copy-done.1
  603.7 329.9 %all-reduce.5.cloned.1.call-done = f32[4,4,16384]{2,1,0:T(4,128)} async-done(((f32[4,4,16384]{2,1,0:T(4,128)}), f32[4,4,16384]{2,1,0:T(4,128)}) %all-reduce.5.cloned.1.call-update) | async-done | bytes 1048592 | tf_op jit(solution)/shard_map/psum | solution.py:54
  933.6 1.5 subtract_convert_fusion
  935.1 36.6 %while.43 = (s32[]{:T(128)}, f32[4,4,512]{2,1,0:T(4,128)S(1)}, s32[]{:T(128)}, s32[8]{0:T(128)S(1)}, s32[8]{0:T(128)S(1)}, /*index=5*/bf16[4,4,16384]{2,1,0:T(4,...) while((s32[]{:T(128)}, f32[4,4,512]{2,1,0:T(4,128)S(1)}, ...), condition=%wide.region_11.12_spmd, body=%wide.region_10.11_spmd.sunk | while | flops 2101261 | bytes 565535 | solution.py:34
  937.1 0.7 dynamic_slice.127
  938.4 1.2 fusion.43
  940.3 0.7 dynamic_slice.128
  941.6 0.7 dynamic_slice.127
  942.9 1.2 fusion.43
  944.8 0.7 dynamic_slice.128
  947.4 1.2 fusion.43
  951.9 1.2 fusion.43
  956.4 1.2 fusion.43
  960.9 1.2 fusion.43
  965.4 1.2 fusion.43
  969.9 1.2 fusion.43
  971.8 8.5 psum.31
  (71 shorter events, 32.4 us)
Async XLA Ops:
  6.5 379.7 %all-reduce.3.cloned.1.call-start = ((), (), s32[]{:S(2)}) async-start(), calls=%async_computation | async-start | bytes 2097152 | tf_op jit(solution)/shard_map/psum | solution.py:54
  45.4 1.0 copy-start
  45.4 511.5 %copy-start.3 = (f32[4,4,512]{2,1,0:T(4,128)S(1)}, f32[4,4,512]{2,1,0:T(4,128)}, u32[]{:S(2)}) copy-start(f32[4,4,512]{2,1,0:T(4,128)} %param.18) | copy-start | bytes 98308
  45.4 520.0 %copy-start.4 = (f32[512]{0:T(512)S(1)}, f32[512]{0:T(512)}, u32[]{:S(2)}) copy-start(f32[512]{0:T(512)} %param.21) | copy-start | bytes 6148
  46.4 472.0 %all-gather.2.cloned.1.call-start = ((), (), s32[]{:S(2)}) async-start(), calls=%async_computation.1 | async-start | bytes 1056768 | tf_op jit(solution)/shard_map/all_gather | solution.py:46
  47.1 886.5 %all-reduce.5.cloned.1.call-start = ((), (), s32[]{:S(2)}) async-start(), calls=%async_computation.2 | async-start | bytes 2097152 | tf_op jit(solution)/shard_map/psum | solution.py:54
  520.2 413.5 %copy-start.2 = (f32[4,4,16384]{2,1,0:T(4,128)S(1)}, f32[4,4,16384]{2,1,0:T(4,128)}, u32[]{:S(2)}) copy-start(f32[4,4,16384]{2,1,0:T(4,128)} %all-gather.2.cloned.1.call-done) | copy-start | bytes 3145732
  602.7 1.0 copy-start.1
Sparse Core Ops, SparseCore 0:
  46.5 339.6 all-reduce.2
  389.6 128.6 all-gather.1
  603.8 329.7 all-reduce.4
where the time goes:
time: 990 us; the launch traced here: 987 us
  waiting for transfers between devices  801 us (81%)
  loops' own time  65.6 us (7%)
  local copies, waits for them, and re-layouts  44 us (4%)
  matrix products  40.3 us (4%)
  blocking collectives  16.9 us (2%)
  between operations  13.9 us (1%)
    psum x2, waiting for transfers between devices, body(): totals = lax.psum(partial_value, 'scan')  668 us
    all_gather x1, waiting for transfers between devices, body(): measured_all = lax.all_gather(measured, 'scan', axis=2, tiled=True)  132 us
    another operation x2, loops' own time, add_forward(): return lax.fori_loop(first_slot, end_slot, advance, partial_value)  32.8 us
    another operation x2, loops' own time, add_backward(): return lax.fori_loop(first_slot, end_slot, advance, gradient)  32.7 us
    dot_general x16, matrix products, advance(): jnp.einsum('fij,fsj->fsi', matrix, source, preferred_element_type=jnp.flo...  20.6 us
  transfers between devices with their start and end apart: 3, of which 3 were waited for; matrix products, arithmetic and copies ran while one was open for 0% of the time, Pallas kernels for 0%

commit v1 on v0

v1 whole, which is shorter than its diff:
```python
import functools

import jax
import jax.numpy as jnp
from jax import lax
from jax.experimental import pallas as pl
from jax.experimental.pallas import tpu as pltpu
from jax.sharding import PartitionSpec as P

ITERS = 2
CORES = 2
ALONG_X = 4
MESH = pl.DeviceIdType.MESH


def kernel(along_z, bins, tiles_hbm, pattern, count, map_ref, measured_ref, step_ref, penalty_ref, out_ref,
           tiles, current, sources, measured, lookup_out, lookup_in, lookup_smem, sums_matrix,
           part_out, part_in, chunk_out, chunk_in, rounded_in, gather_out, gather_in, lhs, energy_out, energy_in,
           tile_sem, smem_sem, send_sem, recv_sem):
    slots, bins_dev, tile, _ = tiles.shape
    group = ALONG_X * CORES
    half = tile // 2
    rows = 16
    snaps = rows // bins_dev
    scan = lax.axis_index("scan")
    y = lax.axis_index("bin")
    core = lax.rem(scan, CORES)
    x = lax.rem(scan // CORES, ALONG_X)
    z = scan // group

    def member(k):
        dx, dc = k // CORES, k % CORES
        there = (z * ALONG_X + lax.rem(x + dx, ALONG_X)) * CORES + (core if dc == 0 else 1 - core)
        return (there, y)

    def along(k):
        return (lax.rem(z + k, along_z) * group + lax.rem(scan, group), y)

    def plane(k):
        return (scan, lax.rem(y + k, bins))

    peers = [member(k) for k in range(1, group)] + [along(k) for k in range(1, along_z)]
    peers += [plane(k) for k in range(1, bins)]
    barrier = pltpu.get_barrier_semaphore()
    for peer in peers:
        pl.semaphore_signal(barrier, inc=1, device_id=peer, device_id_type=MESH)
    loads = []
    for s in range(slots):
        load = pltpu.make_async_copy(tiles_hbm.at[s], tiles.at[s], tile_sem.at[s])
        load.start()
        loads.append(load)

    finish = []

    def exchange(index, src_of, dst, count_, device_of):
        for k in range(1, count_):
            pltpu.make_async_remote_copy(
                src_ref=src_of(k), dst_ref=dst.at[k], send_sem=send_sem.at[index], recv_sem=recv_sem.at[index],
                device_id=device_of(k), device_id_type=MESH,
            ).start()
        whole = dst.at[pl.ds(1, count_ - 1)]
        done = pltpu.make_async_remote_copy(
            src_ref=whole, dst_ref=whole, send_sem=send_sem.at[index], recv_sem=recv_sem.at[index],
            device_id=device_of(1), device_id_type=MESH,
        )
        finish.append(done)
        return done

    lane_slot = lax.broadcasted_iota(jnp.int32, (8, 128), 1) // rows
    names = jnp.zeros((8, 128), jnp.int32)
    live = jnp.zeros((8, 128), jnp.int32)
    for s in range(slots):
        names = jnp.where(lane_slot == s, pattern[0, s], names)
        live = jnp.where(lane_slot == s, (s < count[0]).astype(jnp.int32), live)
    place = lax.rem(z + along_z - names // ALONG_X, along_z)
    for dx in range(ALONG_X):
        there = lax.rem(x + dx, ALONG_X)
        wanted = jnp.where((lax.rem(names, ALONG_X) == there) & (live == 1), place, along_z)
        lookup_out[dx] = wanted
        if dx == 0:
            lookup_in[0] = wanted

    for f in range(bins_dev):
        at = pl.ds(f * snaps, snaps)
        measured[at, :] = measured_ref[f]
        for t in range(2):
            current[t, at, :] = map_ref[f, :, pl.ds(t * tile, tile)]
    row_bin = lax.broadcasted_iota(jnp.int32, (rows, tile), 0) // snaps
    step_size = step_ref[0]
    zeros = jnp.zeros((rows, half), jnp.bfloat16)

    for it in range(ITERS):
        base = 1 + 5 * it
        for t in range(2):
            value = current[t]
            for f in range(bins_dev):
                sources[t, f] = jnp.where(row_bin == f, value, 0.0).astype(jnp.bfloat16)
        own = part_in.at[it]
        out = part_out.at[it]
        for s in range(slots):
            if it == 0:
                loads[s].wait()
            which = lax.rem(pattern[1, s], 2)
            total = jnp.zeros((rows, tile), jnp.float32)
            for f in range(bins_dev):
                total += lax.dot_general(
                    sources[which, f], tiles[s, f], (((1,), (1,)), ((), ())), preferred_element_type=jnp.float32
                )
            low, high = total[:, :half], total[:, half:]
            for dc, value in enumerate((jnp.where(core == 0, low, high), jnp.where(core == 0, high, low))):
                large = value.astype(jnp.bfloat16)
                out[dc, 0, s] = large
                out[dc, 1, s] = (value - large.astype(jnp.float32)).astype(jnp.bfloat16)
        own[0] = out[0]
        if it == 0:
            pl.semaphore_wait(barrier, len(peers))
            told = exchange(0, lambda k: lookup_out.at[k // CORES], lookup_in, group, member)
        parts = exchange(base, lambda k: out.at[k % CORES], own, group, member)
        if it == 0:
            told.wait_recv()
            to_smem = pltpu.make_async_copy(lookup_in, lookup_smem, smem_sem.at[0])
            to_smem.start()
            matrix_row = lax.broadcasted_iota(jnp.int32, (along_z * rows, 128), 0)
            matrix_lane = lax.broadcasted_iota(jnp.int32, (along_z * rows, 128), 1)
            matches = lax.rem(along_z - matrix_row // rows, along_z)
            same = lax.rem(matrix_row, rows) == lax.rem(matrix_lane, rows)
            for k in range(group):
                hit = same & (matches == lookup_in[k, pl.ds(0, 1), :])
                sums_matrix[:, pl.ds(k * 128, 128)] = hit.astype(jnp.float32).astype(jnp.bfloat16)
            to_smem.wait()
        parts.wait_recv()
        chunks = jnp.zeros((along_z * rows, half), jnp.float32)
        for piece in range(2):
            chunks += jnp.dot(
                sums_matrix[...], own[:, piece].reshape(group * slots * rows, half),
                preferred_element_type=jnp.float32,
            )
        chunk_out[it] = chunks.reshape(along_z, rows, half)
        summed = exchange(base + 1, lambda k: chunk_out.at[it, k], chunk_in.at[it], along_z, along)
        total = chunks[:rows] - measured[...]
        summed.wait_recv()
        for k in range(1, along_z):
            total += chunk_in[it, k]
        held = rounded_in.at[it]
        held[0] = total.astype(jnp.bfloat16)
        held[along_z] = zeros
        spread = exchange(base + 2, lambda k: held.at[0], held, along_z, along)
        spread.wait_recv()
        for k in range(group):
            asker = (ALONG_X - k // CORES) % ALONG_X * CORES + k % CORES
            for s in range(slots):
                block = held[lookup_smem[asker, 0, s * rows]]
                if k == 0:
                    gather_in[it, 0, s] = block
                else:
                    gather_out[it, k, s] = block
        gathered = exchange(base + 3, lambda k: gather_out.at[it, k], gather_in.at[it], group, member)
        gathered.wait_recv()
        gradient = jnp.zeros((2 * rows, tile), jnp.float32)
        for s in range(slots):
            which = lax.rem(pattern[1, s], 2)
            mine = gather_in[it, 0, s]
            other = gather_in[it, 1, s]
            for dx in range(1, ALONG_X):
                mine += gather_in[it, dx * CORES, s]
                other += gather_in[it, dx * CORES + 1, s]
            low = jnp.where(core == 0, mine, other).astype(jnp.float32)
            high = jnp.where(core == 0, other, mine).astype(jnp.float32)
            both = jnp.concatenate([low, high], axis=1)
            for f in range(bins_dev):
                one = jnp.where(row_bin == f, both, 0.0)
                for t in range(2):
                    lhs[pl.ds(t * rows, rows), pl.ds(f * tile, tile)] = jnp.where(which == t, one, 0.0).astype(
                        jnp.bfloat16
                    )
            gradient += jnp.dot(
                lhs[...], tiles[s].reshape(bins_dev * tile, tile), preferred_element_type=jnp.float32
            )
        for t in range(2):
            moved = current[t] - step_size * gradient[t * rows:(t + 1) * rows]
            current[t] = moved
            energy_in[it, 0, :, pl.ds(t * tile, tile)] = jnp.sum(moved * moved, axis=0, keepdims=True)
        energy_out[it] = energy_in[it, 0]
        energies = exchange(base + 4, lambda k: energy_out.at[it], energy_in.at[it], bins, plane)
        energies.wait_recv()
        energy = energy_in[it, 0]
        for k in range(1, bins):
            energy += energy_in[it, k]
        factor = jnp.maximum(0.0, 1.0 - step_size * penalty_ref[...] / jnp.sqrt(energy + 1e-06))
        for t in range(2):
            current[t] = current[t] * factor[:, t * tile:(t + 1) * tile]
    for f in range(bins_dev):
        for t in range(2):
            out_ref[f, :, pl.ds(t * tile, tile)] = current[t, pl.ds(f * snaps, snaps), :]
    for done in finish:
        done.wait_send()


def solution(mesh):
    scan, bins = mesh.shape["scan"], mesh.shape["bin"]
    along_z = scan // (ALONG_X * CORES)

    def body(tile_blocks, tile_pattern, tile_count, initial_map, measured, step_size, penalty):
        slots, bins_dev, tile, _ = tile_blocks.shape
        rows, half, group = bins_dev * initial_map.shape[1], tile // 2, ALONG_X * CORES
        points = initial_map.shape[2]
        bf16, f32 = jnp.bfloat16, jnp.float32
        smem = pl.BlockSpec(memory_space=pltpu.SMEM)
        vmem = pl.BlockSpec(memory_space=pltpu.VMEM)
        exchanges = 1 + 5 * ITERS
        return pl.pallas_call(
            functools.partial(kernel, along_z, bins),
            out_shape=jax.ShapeDtypeStruct(initial_map.shape, f32),
            in_specs=[pl.BlockSpec(memory_space=pl.ANY), smem, smem, vmem, vmem, smem, vmem],
            out_specs=vmem,
            scratch_shapes=[
                pltpu.VMEM((slots, bins_dev, tile, tile), bf16),
                pltpu.VMEM((2, rows, tile), f32),
                pltpu.VMEM((2, bins_dev, rows, tile), bf16),
                pltpu.VMEM((rows, half), f32),
                pltpu.VMEM((ALONG_X, 8, 128), jnp.int32),
                pltpu.VMEM((group, 8, 128), jnp.int32),
                pltpu.SMEM((group, 8, 128), jnp.int32),
                pltpu.VMEM((along_z * rows, group * slots * rows), bf16),
                pltpu.VMEM((ITERS, CORES, 2, slots, rows, half), bf16),
                pltpu.VMEM((ITERS, group, 2, slots, rows, half), bf16),
                pltpu.VMEM((ITERS, along_z, rows, half), f32),
                pltpu.VMEM((ITERS, along_z, rows, half), f32),
                pltpu.VMEM((ITERS, along_z + 1, rows, half), bf16),
                pltpu.VMEM((ITERS, group, slots, rows, half), bf16),
                pltpu.VMEM((ITERS, group, slots, rows, half), bf16),
                pltpu.VMEM((2 * rows, bins_dev * tile), bf16),
                pltpu.VMEM((ITERS, 1, points), f32),
                pltpu.VMEM((ITERS, bins, 1, points), f32),
                pltpu.SemaphoreType.DMA((slots,)),
                pltpu.SemaphoreType.DMA((1,)),
                pltpu.SemaphoreType.DMA((exchanges,)),
                pltpu.SemaphoreType.DMA((exchanges,)),
            ],
            compiler_params=pltpu.CompilerParams(
                collective_id=0, has_side_effects=True, vmem_limit_bytes=32 * 1024 * 1024
            ),
        )(tile_blocks, tile_pattern, tile_count, initial_map, measured, step_size, penalty.reshape(1, points))

    in_specs = (
        P("scan", "bin", None, None),
        P(None, "scan"),
        P("scan"),
        P("bin", None, "scan"),
        P("bin", None, "scan"),
        P(),
        P("scan"),
    )
    return jax.shard_map(body, mesh=mesh, in_specs=in_specs, out_specs=P("bin", None, "scan"), check_vma=False)
```

time: 990 us -> 101 us (0.10)
  waiting for transfers between devices: 801 us -> 0 us
  Pallas kernels: 0 us -> 93.8 us
  loops' own time: 65.6 us -> 0 us
  matrix products: 40.3 us -> 0 us
  local copies, waits for them, and re-layouts: 44 us -> 5.61 us
  blocking collectives: 16.9 us -> 0 us
  between operations: 13.9 us -> 1.32 us
    psum x2 -> x0, waiting for transfers between devices: 668 us -> none  [body(): totals = lax.psum(partial_value, 'scan')]
    all_gather x1 -> x0, waiting for transfers between devices: 132 us -> none  [body(): measured_all = lax.all_gather(measured, 'scan', axis=2, tiled=True)]
    pallas_call x0 -> x1, Pallas kernels: none -> 93.8 us  [body(): pl.pallas_call(functools.partial(kernel, along_z, bins), out_shape=jax.Sh...]
    another operation x4 -> x0, loops' own time: 65.6 us -> none  [the longest x2 32.8 us: add_forward(): return lax.fori_loop(first_slot, end_slot, advance, partial_value)]
    dynamic_slice x64 -> x0, local copies, waits for them, and re-layouts: 41.7 us -> none  [the longest x16 10.4 us: advance(): start = block_rows[slot_id] * tile_width]
    dot_general x32 -> x0, matrix products: 40.3 us -> none  [the longest x16 20.6 us: advance(): jnp.einsum('fij,fsj->fsi', matrix, source, preferred_element_type=jnp.flo...]
    psum x2 -> x0, blocking collectives: 16.9 us -> none  [body(): energy = lax.psum(jnp.sum(moved * moved, axis=(0, 1)), 'bin')]
  transfers between devices with their start and end apart: 3 -> 0, of which waited for: 3 -> 0; matrix products, arithmetic and copies ran while one was open for 0% -> 0% of each run, Pallas kernels for 0% -> 0%
where the time goes in v1:
time: 101 us
  Pallas kernels  93.8 us (93%)
  local copies, waits for them, and re-layouts  5.61 us (6%)
  between operations  1.32 us (1%)
    pallas_call x1, Pallas kernels, body(): pl.pallas_call(functools.partial(kernel, along_z, bins), out_shape=jax.Sh...  93.8 us
    unnamed x11, local copies, waits for them, and re-layouts  5.61 us

profile of v1, /device:TPU:1, one launch (start us, length us, event | category | flops | bytes accessed | tf_op | source)
XLA Modules:
  0.0 100.7 jit_solution(11601866810674444612)
XLA Ops:
  1.3 0.0 copy-start
  1.3 2.2 %copy-done = bf16[8,4,256,256]{3,2,1,0:T(8,128)(2,1)S(1)} copy-done((bf16[8,4,256,256]{3,2,1,0:T(8,128)(2,1)S(1)}, bf16[8,4,256,256]{3,2,1,0:T(8,128)(2,1)}, u32[]{:S(2)}) %copy-start) | copy-done | bytes 4194328
  3.5 0.0 copy-start.1
  3.5 0.8 copy-done.1
  4.2 0.0 copy-start.2
  4.2 0.7 copy-done.2
  4.9 0.0 copy-start.3
  4.9 0.7 copy-done.3
  5.6 0.0 copy-start.4
  5.6 0.7 copy-done.4
  6.3 93.8 %shard_map.73 = f32[4,4,512]{2,1,0:T(4,128)S(1)} custom-call(bf16[8,4,256,256]{3,2,1,0:T(8,128)(2,1)S(1)} %copy-done, s32[2,8]{1,0:T(2,128)S(1)} %copy-done.4, s32[1]{0:T(128)S(6)} %copy.9.count, f32[4,4,512]{2,1,0:T(4,128)S(1)} %copy-done.1, f32[4,4,128]{2,1,0:T(4,128)S(1)} %copy-done.2, f32[1]{0:T(128)S(6)} %copy.10.step_ref, f32[1,512]{1,0:T(1,128)S(1)} %bitcast.1), custom_call_target="tpu_custom_call" | custom-call | tf_op jit(solution)/shard_map/pallas_call | solution.py:211
  100.1 0.6 copy.11
Async XLA Ops:
  1.3 2.2 %copy-start = (bf16[8,4,256,256]{3,2,1,0:T(8,128)(2,1)S(1)}, bf16[8,4,256,256]{3,2,1,0:T(8,128)(2,1)}, u32[]{:S(2)}) copy-start(bf16[8,4,256,256]{3,2,1,0:T(8,128)(2,1)} %tiles_hbm.1) | copy-start | bytes 12582916
  3.5 0.8 copy-start.1
  4.2 0.7 copy-start.2
  4.9 0.7 copy-start.3
  5.6 0.7 copy-start.4

commit v2 on v1

--- a/solution.py
+++ b/solution.py
@@ -13,10 +13,10 @@
 MESH = pl.DeviceIdType.MESH
 
 
-def kernel(along_z, bins, tiles_hbm, pattern, count, map_ref, measured_ref, step_ref, penalty_ref, out_ref,
-           tiles, current, sources, measured, lookup_out, lookup_in, lookup_smem, sums_matrix,
+def kernel(along_z, bins, tiles_hbm, pattern_hbm, count, map_hbm, measured_hbm, step_ref, penalty_hbm, out_ref,
+           pattern, map_ref, measured_ref, penalty_ref, tiles, current, sources, measured, lookup_out, lookup_in, lookup_smem, sums_matrix,
            part_out, part_in, chunk_out, chunk_in, rounded_in, gather_out, gather_in, lhs, energy_out, energy_in,
-           tile_sem, smem_sem, send_sem, recv_sem):
+           tile_sem, input_sem, smem_sem, send_sem, recv_sem):
     slots, bins_dev, tile, _ = tiles.shape
     group = ALONG_X * CORES
     half = tile // 2
@@ -39,8 +39,17 @@
     def plane(k):
         return (scan, lax.rem(y + k, bins))
 
-    peers = [member(k) for k in range(1, group)] + [along(k) for k in range(1, along_z)]
-    peers += [plane(k) for k in range(1, bins)]
+    z_order = sorted(range(1, along_z), key=lambda k: -min(k, along_z - k))
+    group_order = sorted(range(1, group), key=lambda k: (-min(k // CORES, ALONG_X - k // CORES), -(k % CORES)))
+    plane_order = sorted(range(1, bins), key=lambda k: -min(k, bins - k))
+    peers = [along(k) for k in z_order] + [member(k) for k in group_order] + [plane(k) for k in plane_order]
+    inputs = []
+    for i, (there, here) in enumerate((
+        (pattern_hbm, pattern), (map_hbm, map_ref), (measured_hbm, measured_ref), (penalty_hbm, penalty_ref),
+    )):
+        load = pltpu.make_async_copy(there, here, input_sem.at[i])
+        load.start()
+        inputs.append(load)
     barrier = pltpu.get_barrier_semaphore()
     for peer in peers:
         pl.semaphore_signal(barrier, inc=1, device_id=peer, device_id_type=MESH)
@@ -50,15 +59,17 @@
         load.start()
         loads.append(load)
 
+    for load in inputs:
+        load.wait()
     finish = []
 
-    def exchange(index, src_of, dst, count_, device_of):
-        for k in range(1, count_):
+    def exchange(index, src_of, dst, order, device_of):
+        for k in order:
             pltpu.make_async_remote_copy(
                 src_ref=src_of(k), dst_ref=dst.at[k], send_sem=send_sem.at[index], recv_sem=recv_sem.at[index],
                 device_id=device_of(k), device_id_type=MESH,
             ).start()
-        whole = dst.at[pl.ds(1, count_ - 1)]
+        whole = dst.at[pl.ds(1, len(order))]
         done = pltpu.make_async_remote_copy(
             src_ref=whole, dst_ref=whole, send_sem=send_sem.at[index], recv_sem=recv_sem.at[index],
             device_id=device_of(1), device_id_type=MESH,
@@ -109,13 +120,13 @@
             low, high = total[:, :half], total[:, half:]
             for dc, value in enumerate((jnp.where(core == 0, low, high), jnp.where(core == 0, high, low))):
                 large = value.astype(jnp.bfloat16)
-                out[dc, 0, s] = large
-                out[dc, 1, s] = (value - large.astype(jnp.float32)).astype(jnp.bfloat16)
+                out[dc, s, :, pl.ds(0, half)] = large
+                out[dc, s, :, pl.ds(half, half)] = (value - large.astype(jnp.float32)).astype(jnp.bfloat16)
         own[0] = out[0]
         if it == 0:
             pl.semaphore_wait(barrier, len(peers))
-            told = exchange(0, lambda k: lookup_out.at[k // CORES], lookup_in, group, member)
-        parts = exchange(base, lambda k: out.at[k % CORES], own, group, member)
+            told = exchange(0, lambda k: lookup_out.at[k // CORES], lookup_in, group_order, member)
+        parts = exchange(base, lambda k: out.at[k % CORES], own, group_order, member)
         if it == 0:
             told.wait_recv()
             to_smem = pltpu.make_async_copy(lookup_in, lookup_smem, smem_sem.at[0])
@@ -129,14 +140,12 @@
                 sums_matrix[:, pl.ds(k * 128, 128)] = hit.astype(jnp.float32).astype(jnp.bfloat16)
             to_smem.wait()
         parts.wait_recv()
-        chunks = jnp.zeros((along_z * rows, half), jnp.float32)
-        for piece in range(2):
-            chunks += jnp.dot(
-                sums_matrix[...], own[:, piece].reshape(group * slots * rows, half),
-                preferred_element_type=jnp.float32,
-            )
+        chunks = jnp.dot(
+            sums_matrix[...], own[...].reshape(group * slots * rows, tile), preferred_element_type=jnp.float32
+        )
+        chunks = chunks[:, :half] + chunks[:, half:]
         chunk_out[it] = chunks.reshape(along_z, rows, half)
-        summed = exchange(base + 1, lambda k: chunk_out.at[it, k], chunk_in.at[it], along_z, along)
+        summed = exchange(base + 1, lambda k: chunk_out.at[it, k], chunk_in.at[it], z_order, along)
         total = chunks[:rows] - measured[...]
         summed.wait_recv()
         for k in range(1, along_z):
@@ -144,7 +153,7 @@
         held = rounded_in.at[it]
         held[0] = total.astype(jnp.bfloat16)
         held[along_z] = zeros
-        spread = exchange(base + 2, lambda k: held.at[0], held, along_z, along)
+        spread = exchange(base + 2, lambda k: held.at[0], held, z_order, along)
         spread.wait_recv()
         for k in range(group):
             asker = (ALONG_X - k // CORES) % ALONG_X * CORES + k % CORES
@@ -154,7 +163,7 @@
                     gather_in[it, 0, s] = block
                 else:
                     gather_out[it, k, s] = block
-        gathered = exchange(base + 3, lambda k: gather_out.at[it, k], gather_in.at[it], group, member)
+        gathered = exchange(base + 3, lambda k: gather_out.at[it, k], gather_in.at[it], group_order, member)
         gathered.wait_recv()
         gradient = jnp.zeros((2 * rows, tile), jnp.float32)
         for s in range(slots):
@@ -181,7 +190,7 @@
             current[t] = moved
             energy_in[it, 0, :, pl.ds(t * tile, tile)] = jnp.sum(moved * moved, axis=0, keepdims=True)
         energy_out[it] = energy_in[it, 0]
-        energies = exchange(base + 4, lambda k: energy_out.at[it], energy_in.at[it], bins, plane)
+        energies = exchange(base + 4, lambda k: energy_out.at[it], energy_in.at[it], plane_order, plane)
         energies.wait_recv()
         energy = energy_in[it, 0]
         for k in range(1, bins):
@@ -205,15 +214,18 @@
         rows, half, group = bins_dev * initial_map.shape[1], tile // 2, ALONG_X * CORES
         points = initial_map.shape[2]
         bf16, f32 = jnp.bfloat16, jnp.float32
-        smem = pl.BlockSpec(memory_space=pltpu.SMEM)
-        vmem = pl.BlockSpec(memory_space=pltpu.VMEM)
         exchanges = 1 + 5 * ITERS
+        hbm, smem = pl.BlockSpec(memory_space=pltpu.HBM), pl.BlockSpec(memory_space=pltpu.SMEM)
         return pl.pallas_call(
             functools.partial(kernel, along_z, bins),
             out_shape=jax.ShapeDtypeStruct(initial_map.shape, f32),
-            in_specs=[pl.BlockSpec(memory_space=pl.ANY), smem, smem, vmem, vmem, smem, vmem],
-            out_specs=vmem,
+            in_specs=[hbm, hbm, smem, hbm, hbm, smem, hbm],
+            out_specs=pl.BlockSpec(memory_space=pltpu.VMEM),
             scratch_shapes=[
+                pltpu.SMEM(tile_pattern.shape, jnp.int32),
+                pltpu.VMEM(initial_map.shape, f32),
+                pltpu.VMEM(measured.shape, f32),
+                pltpu.VMEM((1, points), f32),
                 pltpu.VMEM((slots, bins_dev, tile, tile), bf16),
                 pltpu.VMEM((2, rows, tile), f32),
                 pltpu.VMEM((2, bins_dev, rows, tile), bf16),
@@ -222,8 +234,8 @@
                 pltpu.VMEM((group, 8, 128), jnp.int32),
                 pltpu.SMEM((group, 8, 128), jnp.int32),
                 pltpu.VMEM((along_z * rows, group * slots * rows), bf16),
-                pltpu.VMEM((ITERS, CORES, 2, slots, rows, half), bf16),
-                pltpu.VMEM((ITERS, group, 2, slots, rows, half), bf16),
+                pltpu.VMEM((ITERS, CORES, slots, rows, tile), bf16),
+                pltpu.VMEM((ITERS, group, slots, rows, tile), bf16),
                 pltpu.VMEM((ITERS, along_z, rows, half), f32),
                 pltpu.VMEM((ITERS, along_z, rows, half), f32),
                 pltpu.VMEM((ITERS, along_z + 1, rows, half), bf16),
@@ -233,12 +245,13 @@
                 pltpu.VMEM((ITERS, 1, points), f32),
                 pltpu.VMEM((ITERS, bins, 1, points), f32),
                 pltpu.SemaphoreType.DMA((slots,)),
+                pltpu.SemaphoreType.DMA((4,)),
                 pltpu.SemaphoreType.DMA((1,)),
                 pltpu.SemaphoreType.DMA((exchanges,)),
                 pltpu.SemaphoreType.DMA((exchanges,)),
             ],
             compiler_params=pltpu.CompilerParams(
-                collective_id=0, has_side_effects=True, vmem_limit_bytes=32 * 1024 * 1024
+                collective_id=0, has_side_effects=True, vmem_limit_bytes=56 * 1024 * 1024
             ),
         )(tile_blocks, tile_pattern, tile_count, initial_map, measured, step_size, penalty.reshape(1, points))
 

time: 101 us -> 86.3 us (0.85)
  Pallas kernels: 93.8 us -> 83 us
  local copies, waits for them, and re-layouts: 5.61 us -> 1.38 us
    pallas_call x1, Pallas kernels: 93.8 us -> 83 us  [body(): pl.pallas_call(functools.partial(kernel, along_z, bins), out_shape=jax.Sh...]
    unnamed x11 -> x1, local copies, waits for them, and re-layouts: 5.61 us -> 1.38 us
where the time goes in v2:
time: 86.3 us; the launch traced here: 85.7 us
  Pallas kernels  83 us (96%)
  local copies, waits for them, and re-layouts  1.38 us (2%)
  between operations  1.3 us (2%)
    pallas_call x1, Pallas kernels, body(): pl.pallas_call(functools.partial(kernel, along_z, bins), out_shape=jax.Sh...  83 us

profile of v2, /device:TPU:1, one launch (start us, length us, event | category | flops | bytes accessed | tf_op | source)
XLA Modules:
  0.0 85.7 jit_solution(14046678281913643423)
XLA Ops:
  1.3 83.0 %shard_map.73 = f32[4,4,512]{2,1,0:T(4,128)} custom-call(bf16[8,4,256,256]{3,2,1,0:T(8,128)(2,1)} %tiles_hbm.1, s32[2,8]{1,0:T(2,128)} %pattern_hbm.1, s32[1]{0:T(128)S(6)} %copy.9.count, f32[4,4,512]{2,1,0:T(4,128)} %map_hbm.1, f32[4,4,128]{2,1,0:T(4,128)} %measured_hbm.1, f32[1]{0:T(128)S(6)} %copy.10.step_ref, f32[1,512]{1,0:T(1,128)} %bitcast.1), custom_call_target="tpu_custom_call" | custom-call | tf_op jit(solution)/shard_map/pallas_call | solution.py:219
  84.3 1.4 %copy.11 = f32[4,4,512]{2,1,0:T(4,128)} copy(f32[4,4,512]{2,1,0:T(4,128)} %shard_map.73) | data formatting | bytes 65536

commit v3 on v2

v3 whole, which is shorter than its diff:
```python
import functools

import jax
import jax.numpy as jnp
from jax import lax
from jax.experimental import pallas as pl
from jax.experimental.pallas import tpu as pltpu
from jax.sharding import PartitionSpec as P

ITERS = 2
CORES = 2
ALONG_X = 4
MESH = pl.DeviceIdType.MESH
LEVELS = 8000.0
BATCHES = 1


def kernel(along_z, bins, tiles_hbm, pattern_hbm, count, map_hbm, measured_hbm, step_ref, penalty_hbm, out_ref,
           pattern, map_ref, measured_ref, penalty_ref, tiles, turned, current, sources, measured, lookup_out, lookup_in, lookup_smem, sums_matrix,
           part_out, part_in, pieces, chunk_out, chunk_in, rounded_in, gather_out, gather_in, energy_out, energy_in,
           tile_sem, input_sem, smem_sem, send_sem, recv_sem):
    slots, bins_dev, tile, _ = tiles.shape
    group = ALONG_X * CORES
    half = tile // 2
    rows = 16
    snaps = rows // bins_dev
    few = slots // BATCHES
    scan = lax.axis_index("scan")
    y = lax.axis_index("bin")
    core = lax.rem(scan, CORES)
    x = lax.rem(scan // CORES, ALONG_X)
    z = scan // group

    def member(k):
        dx, dc = k // CORES, k % CORES
        there = (z * ALONG_X + lax.rem(x + dx, ALONG_X)) * CORES + (core if dc == 0 else 1 - core)
        return (there, y)

    def along(k):
        return (lax.rem(z + k, along_z) * group + lax.rem(scan, group), y)

    def plane(k):
        return (scan, lax.rem(y + k, bins))

    z_order = sorted(range(1, along_z), key=lambda k: -min(k, along_z - k))
    group_order = sorted(range(1, group), key=lambda k: (-min(k // CORES, ALONG_X - k // CORES), -(k % CORES)))
    plane_order = sorted(range(1, bins), key=lambda k: -min(k, bins - k))
    along_at = {k: along(k) for k in z_order}
    member_at = {k: member(k) for k in group_order}
    plane_at = {k: plane(k) for k in plane_order}
    peers = list(along_at.values()) + list(member_at.values()) + list(plane_at.values())
    barrier = pltpu.get_barrier_semaphore()
    for peer in peers:
        pl.semaphore_signal(barrier, inc=1, device_id=peer, device_id_type=MESH)
    inputs = []
    for i, (there, here) in enumerate((
        (pattern_hbm, pattern), (map_hbm, map_ref), (measured_hbm, measured_ref), (penalty_hbm, penalty_ref),
    )):
        load = pltpu.make_async_copy(there, here, input_sem.at[i])
        load.start()
        inputs.append(load)
    loads = []
    for s in range(slots):
        load = pltpu.make_async_copy(tiles_hbm.at[s], tiles.at[s], tile_sem.at[s])
        load.start()
        loads.append(load)

    for load in inputs:
        load.wait()
    finish = []

    sems = iter(range(send_sem.shape[0]))

    def exchange(parts, src_of, dst, devices):
        arrivals = []
        for part in parts:
            sem = next(sems)
            for k in part:
                pltpu.make_async_remote_copy(
                    src_ref=src_of(k), dst_ref=dst.at[k], send_sem=send_sem.at[sem], recv_sem=recv_sem.at[sem],
                    device_id=devices[k], device_id_type=MESH,
                ).start()
            whole = dst.at[pl.ds(min(part), len(part))]
            arrivals.append(pltpu.make_async_remote_copy(
                src_ref=whole, dst_ref=whole, send_sem=send_sem.at[sem], recv_sem=recv_sem.at[sem],
                device_id=devices[part[0]], device_id_type=MESH,
            ))
        finish.extend(arrivals)
        return arrivals

    lane_slot = lax.broadcasted_iota(jnp.int32, (8, 128), 1) // rows
    names = jnp.zeros((8, 128), jnp.int32)
    live = jnp.zeros((8, 128), jnp.int32)
    for s in range(slots):
        names = jnp.where(lane_slot == s, pattern[0, s], names)
        live = jnp.where(lane_slot == s, (s < count[0]).astype(jnp.int32), live)
    place = lax.rem(z + along_z - names // ALONG_X, along_z)
    for dx in range(ALONG_X):
        there = lax.rem(x + dx, ALONG_X)
        wanted = jnp.where((lax.rem(names, ALONG_X) == there) & (live == 1), place, along_z)
        lookup_out[dx] = wanted
        if dx == 0:
            lookup_in[0] = wanted

    for f in range(bins_dev):
        at = pl.ds(f * snaps, snaps)
        measured[at, :] = measured_ref[f]
        for t in range(2):
            current[t, at, :] = map_ref[f, :, pl.ds(t * tile, tile)]
    row_bin = lax.broadcasted_iota(jnp.int32, (rows, tile), 0) // snaps
    step_size = step_ref[0]
    zeros = jnp.zeros((rows, half), jnp.bfloat16)
    lane = lax.broadcasted_iota(jnp.int32, (rows, 128), 1)

    def split(k, s, value):
        at = pl.ds((k * slots + s) * rows, rows)
        large = value.astype(jnp.bfloat16)
        pieces[at, pl.ds(0, half)] = large
        pieces[at, pl.ds(half, half)] = (value - large.astype(jnp.float32)).astype(jnp.bfloat16)


    for it in range(ITERS):
        for t in range(2):
            value = current[t]
            for f in range(bins_dev):
                sources[t, f] = jnp.where(row_bin == f, value, 0.0).astype(jnp.bfloat16)
        own, out = part_in.at[it], part_out.at[it]
        outer = [[k, k + 1] for k in range(CORES, group, CORES)]
        outer = sorted(outer, key=lambda part: group_order.index(part[1])) + [[1]]
        arrivals = []
        for batch in range(BATCHES):
            powers = jnp.zeros((rows, 128), jnp.float32)
            for i in range(few):
                s = batch * few + i
                if it == 0:
                    loads[s].wait()
                which = lax.rem(pattern[1, s], 2)
                total = jnp.zeros((rows, tile), jnp.float32)
                for f in range(bins_dev if it == 0 else 0):
                    total += lax.dot_general(
                        sources[which, f], tiles[s, f], (((1,), (1,)), ((), ())), preferred_element_type=jnp.float32
                    )
                if it > 0:
                    wide = jnp.concatenate([sources[which, f] for f in range(bins_dev)], axis=1)
                    total = jnp.dot(wide, turned[s], preferred_element_type=jnp.float32)
                largest = jnp.max(jnp.abs(total), axis=1, keepdims=True)
                power = jnp.clip(jnp.ceil(jnp.log2(jnp.maximum(largest, 1e-30))), -100.0, 126.0)
                powers = jnp.where(lane == i, power, powers)
                low, high = total[:, :half], total[:, half:]
                mine, other = jnp.where(core == 0, low, high), jnp.where(core == 0, high, low)
                split(0, s, mine)
                for dc, value in enumerate((mine, other)):
                    out[batch, dc, i] = jnp.round(value * (jnp.exp2(-power) * LEVELS)).astype(jnp.int32).astype(jnp.int16)
            for dc in range(CORES):
                out[batch, dc, few] = powers.astype(jnp.int32).astype(jnp.int16)
            if it == 0 and batch < BATCHES - 1:
                continue
            if it == 0:
                pl.semaphore_wait(barrier, len(peers))
                (told,) = exchange([group_order], lambda k: lookup_out.at[k // CORES], lookup_in, member_at)
            for sent in (range(BATCHES) if it == 0 else [batch]):
                arrivals.append(exchange(outer, lambda k: out.at[sent, k % CORES], own.at[sent], member_at))
        if it == 0:
            told.wait_recv()
            to_smem = pltpu.make_async_copy(lookup_in, lookup_smem, smem_sem.at[0])
            to_smem.start()
            matrix_row = lax.broadcasted_iota(jnp.int32, (along_z * rows, 128), 0)
            matrix_lane = lax.broadcasted_iota(jnp.int32, (along_z * rows, 128), 1)
            matches = lax.rem(along_z - matrix_row // rows, along_z)
            same = lax.rem(matrix_row, rows) == lax.rem(matrix_lane, rows)
            for k in range(group):
                hit = same & (matches == lookup_in[k, pl.ds(0, 1), :])
                sums_matrix[:, pl.ds(k * 128, 128)] = hit.astype(jnp.float32).astype(jnp.bfloat16)
        chunks = jnp.zeros((along_z * rows, tile), jnp.float32)
        for batch in range(BATCHES):
            for part, arrival in reversed(list(zip(outer, arrivals[batch]))):
                arrival.wait_recv()
                for k in part:
                    scale = jnp.exp2(own[batch, k, few].astype(jnp.int32).astype(jnp.float32)) * (1.0 / LEVELS)
                    for i in range(few):
                        value = own[batch, k, i].astype(jnp.int32).astype(jnp.float32)
                        split(k, batch * few + i, value * scale[:, i:i + 1])
                if batch == BATCHES - 1:
                    first, width = min(part) // CORES * CORES * slots * rows, CORES * slots * rows
                    chunks += jnp.dot(
                        sums_matrix[:, pl.ds(first, width)], pieces[pl.ds(first, width), :],
                        preferred_element_type=jnp.float32,
                    )
        chunks = chunks[:, :half] + chunks[:, half:]
        chunk_out[it] = chunks.reshape(along_z, rows, half)
        (summed,) = exchange([z_order], lambda k: chunk_out.at[it, k], chunk_in.at[it], along_at)
        total = chunks[:rows] - measured[...]
        if it == 0:
            for s in range(slots):
                for f in range(bins_dev):
                    turned[s, pl.ds(f * tile, tile), :] = tiles[s, f].T
        summed.wait_recv()
        for k in range(1, along_z):
            total += chunk_in[it, k]
        held = rounded_in.at[it]
        held[0] = total.astype(jnp.bfloat16)
        held[along_z] = zeros
        (spread,) = exchange([z_order], lambda k: held.at[0], held, along_at)
        spread.wait_recv()
        if it == 0:
            to_smem.wait()
        arrivals = []
        for batch in range(BATCHES):

            def gather(k):
                asker = (ALONG_X - k // CORES) % ALONG_X * CORES + k % CORES
                there = (gather_out if k else gather_in).at[it, batch, k]
                for i in range(few):
                    there[i] = held[lookup_smem[asker, 0, (batch * few + i) * rows]]
                return there

            arrivals += exchange([group_order], gather, gather_in.at[it, batch], member_at)
            gather(0)
        gradient = [jnp.zeros((rows, tile), jnp.float32) for t in range(2)]
        for s in range(slots):
            batch, i = s // few, s % few
            if i == 0:
                arrivals[batch].wait_recv()
            which = lax.rem(pattern[1, s], 2)
            mine = gather_in[it, batch, 0, i]
            other = gather_in[it, batch, 1, i]
            for dx in range(1, ALONG_X):
                mine += gather_in[it, batch, dx * CORES, i]
                other += gather_in[it, batch, dx * CORES + 1, i]
            low = jnp.where(core == 0, mine, other).astype(jnp.float32)
            high = jnp.where(core == 0, other, mine).astype(jnp.float32)
            both = jnp.concatenate([low, high], axis=1)
            wide = jnp.concatenate([jnp.where(row_bin == f, both, 0.0) for f in range(bins_dev)], axis=1)
            product = jnp.dot(
                wide.astype(jnp.bfloat16), tiles[s].reshape(bins_dev * tile, tile), preferred_element_type=jnp.float32
            )
            for t in range(2):
                gradient[t] += jnp.where(which == t, product, 0.0)
        for t in range(2):
            moved = current[t] - step_size * gradient[t]
            current[t] = moved
            energy_in[it, 0, :, pl.ds(t * tile, tile)] = jnp.sum(moved * moved, axis=0, keepdims=True)
        energy_out[it] = energy_in[it, 0]
        (energies,) = exchange([plane_order], lambda k: energy_out.at[it], energy_in.at[it], plane_at)
        energies.wait_recv()
        energy = energy_in[it, 0]
        for k in range(1, bins):
            energy += energy_in[it, k]
        factor = jnp.maximum(0.0, 1.0 - step_size * penalty_ref[...] / jnp.sqrt(energy + 1e-06))
        for t in range(2):
            current[t] = current[t] * factor[:, t * tile:(t + 1) * tile]
    for f in range(bins_dev):
        for t in range(2):
            out_ref[f, :, pl.ds(t * tile, tile)] = current[t, pl.ds(f * snaps, snaps), :]
    for done in finish:
        done.wait_send()


def solution(mesh):
    scan, bins = mesh.shape["scan"], mesh.shape["bin"]
    along_z = scan // (ALONG_X * CORES)

    def body(tile_blocks, tile_pattern, tile_count, initial_map, measured, step_size, penalty):
        slots, bins_dev, tile, _ = tile_blocks.shape
        rows, half, group = bins_dev * initial_map.shape[1], tile // 2, ALONG_X * CORES
        points, few = initial_map.shape[2], slots // BATCHES
        bf16, f32 = jnp.bfloat16, jnp.float32
        exchanges = 1 + ((ALONG_X + 1) * BATCHES + 3) * ITERS
        hbm, smem = pl.BlockSpec(memory_space=pltpu.HBM), pl.BlockSpec(memory_space=pltpu.SMEM)
        return pl.pallas_call(
            functools.partial(kernel, along_z, bins),
            out_shape=jax.ShapeDtypeStruct(initial_map.shape, f32),
            in_specs=[hbm, hbm, smem, hbm, hbm, smem, hbm],
            out_specs=pl.BlockSpec(memory_space=pltpu.VMEM),
            scratch_shapes=[
                pltpu.SMEM(tile_pattern.shape, jnp.int32),
                pltpu.VMEM(initial_map.shape, f32),
                pltpu.VMEM(measured.shape, f32),
                pltpu.VMEM((1, points), f32),
                pltpu.VMEM((slots, bins_dev, tile, tile), bf16),
                pltpu.VMEM((slots, bins_dev * tile, tile), bf16),
                pltpu.VMEM((2, rows, tile), f32),
                pltpu.VMEM((2, bins_dev, rows, tile), bf16),
                pltpu.VMEM((rows, half), f32),
                pltpu.VMEM((ALONG_X, 8, 128), jnp.int32),
                pltpu.VMEM((group, 8, 128), jnp.int32),
                pltpu.SMEM((group, 8, 128), jnp.int32),
                pltpu.VMEM((along_z * rows, group * slots * rows), bf16),
                pltpu.VMEM((ITERS, BATCHES, CORES, few + 1, rows, half), jnp.int16),
                pltpu.VMEM((ITERS, BATCHES, group, few + 1, rows, half), jnp.int16),
                pltpu.VMEM((group * slots * rows, tile), bf16),
                pltpu.VMEM((ITERS, along_z, rows, half), f32),
                pltpu.VMEM((ITERS, along_z, rows, half), f32),
                pltpu.VMEM((ITERS, along_z + 1, rows, half), bf16),
                pltpu.VMEM((ITERS, BATCHES, group, few, rows, half), bf16),
                pltpu.VMEM((ITERS, BATCHES, group, few, rows, half), bf16),
                pltpu.VMEM((ITERS, 1, points), f32),
                pltpu.VMEM((ITERS, bins, 1, points), f32),
                pltpu.SemaphoreType.DMA((slots,)),
                pltpu.SemaphoreType.DMA((4,)),
                pltpu.SemaphoreType.DMA((1,)),
                pltpu.SemaphoreType.DMA((exchanges,)),
                pltpu.SemaphoreType.DMA((exchanges,)),
            ],
            compiler_params=pltpu.CompilerParams(
                collective_id=0, has_side_effects=True, vmem_limit_bytes=56 * 1024 * 1024
            ),
        )(tile_blocks, tile_pattern, tile_count, initial_map, measured, step_size, penalty.reshape(1, points))

    in_specs = (
        P("scan", "bin", None, None),
        P(None, "scan"),
        P("scan"),
        P("bin", None, "scan"),
        P("bin", None, "scan"),
        P(),
        P("scan"),
    )
    return jax.shard_map(body, mesh=mesh, in_specs=in_specs, out_specs=P("bin", None, "scan"), check_vma=False)
```

time: 86.3 us -> 81.7 us (0.947)
  Pallas kernels: 83 us -> 78.8 us
    pallas_call x1, Pallas kernels: 83 us -> 78.8 us  [body(): pl.pallas_call(functools.partial(kernel, along_z, bins), out_shape=jax.Sh...]
where the time goes in v3:
time: 81.7 us; the launch traced here: 81.5 us
  Pallas kernels  78.8 us (96%)
  local copies, waits for them, and re-layouts  1.38 us (2%)
  between operations  1.3 us (2%)
    pallas_call x1, Pallas kernels, body(): pl.pallas_call(functools.partial(kernel, along_z, bins), out_shape=jax.Sh...  78.8 us

profile of v3, /device:TPU:1, one launch (start us, length us, event | category | flops | bytes accessed | tf_op | source)
XLA Modules:
  0.0 81.5 jit_solution(7937602150655368641)
XLA Ops:
  1.3 78.8 %shard_map.73 = f32[4,4,512]{2,1,0:T(4,128)} custom-call(bf16[8,4,256,256]{3,2,1,0:T(8,128)(2,1)} %tiles_hbm.1, s32[2,8]{1,0:T(2,128)} %pattern_hbm.1, s32[1]{0:T(128)S(6)} %copy.9.count, f32[4,4,512]{2,1,0:T(4,128)} %map_hbm.1, f32[4,4,128]{2,1,0:T(4,128)} %measured_hbm.1, f32[1]{0:T(128)S(6)} %copy.10.step_ref, f32[1,512]{1,0:T(1,128)} %bitcast.1), custom_call_target="tpu_custom_call" | custom-call | tf_op jit(solution)/shard_map/pallas_call | solution.py:270
  80.1 1.4 %copy.11 = f32[4,4,512]{2,1,0:T(4,128)} copy(f32[4,4,512]{2,1,0:T(4,128)} %shard_map.73) | data formatting | bytes 65536

commit v4 on v3

--- a/solution.py
+++ b/solution.py
@@ -11,7 +11,7 @@
 CORES = 2
 ALONG_X = 4
 MESH = pl.DeviceIdType.MESH
-LEVELS = 8000.0
+LEVELS = 14.9
 BATCHES = 1
 
 
@@ -144,13 +144,13 @@
                     wide = jnp.concatenate([sources[which, f] for f in range(bins_dev)], axis=1)
                     total = jnp.dot(wide, turned[s], preferred_element_type=jnp.float32)
                 largest = jnp.max(jnp.abs(total), axis=1, keepdims=True)
-                power = jnp.clip(jnp.ceil(jnp.log2(jnp.maximum(largest, 1e-30))), -100.0, 126.0)
+                power = jnp.clip(jnp.ceil(jnp.log2(jnp.maximum(largest, 1e-30))), -100.0, 128.0)
                 powers = jnp.where(lane == i, power, powers)
                 low, high = total[:, :half], total[:, half:]
                 mine, other = jnp.where(core == 0, low, high), jnp.where(core == 0, high, low)
                 split(0, s, mine)
                 for dc, value in enumerate((mine, other)):
-                    out[batch, dc, i] = jnp.round(value * (jnp.exp2(-power) * LEVELS)).astype(jnp.int32).astype(jnp.int16)
+                    out[batch, dc, i] = jnp.round(value * jnp.exp2(LEVELS - power)).astype(jnp.int32).astype(jnp.int16)
             for dc in range(CORES):
                 out[batch, dc, few] = powers.astype(jnp.int32).astype(jnp.int16)
             if it == 0 and batch < BATCHES - 1:
@@ -176,7 +176,7 @@
             for part, arrival in reversed(list(zip(outer, arrivals[batch]))):
                 arrival.wait_recv()
                 for k in part:
-                    scale = jnp.exp2(own[batch, k, few].astype(jnp.int32).astype(jnp.float32)) * (1.0 / LEVELS)
+                    scale = jnp.exp2(own[batch, k, few].astype(jnp.int32).astype(jnp.float32) - LEVELS)
                     for i in range(few):
                         value = own[batch, k, i].astype(jnp.int32).astype(jnp.float32)
                         split(k, batch * few + i, value * scale[:, i:i + 1])
@@ -186,10 +186,13 @@
                         sums_matrix[:, pl.ds(first, width)], pieces[pl.ds(first, width), :],
                         preferred_element_type=jnp.float32,
                     )
-        chunks = chunks[:, :half] + chunks[:, half:]
-        chunk_out[it] = chunks.reshape(along_z, rows, half)
-        (summed,) = exchange([z_order], lambda k: chunk_out.at[it, k], chunk_in.at[it], along_at)
-        total = chunks[:rows] - measured[...]
+
+        def give(k):
+            chunk_out[it, k] = chunks[k * rows:(k + 1) * rows, :half] + chunks[k * rows:(k + 1) * rows, half:]
+            return chunk_out.at[it, k]
+
+        (summed,) = exchange([z_order], give, chunk_in.at[it], along_at)
+        total = chunks[:rows, :half] + chunks[:rows, half:] - measured[...]
         if it == 0:
             for s in range(slots):
                 for f in range(bins_dev):

time: 81.7 us -> 81.6 us (level)
  no operation moved by 1% of the time
where the time goes in v4:
time: 81.6 us; the launch traced here: 81.4 us
  Pallas kernels  78.7 us (96%)
  local copies, waits for them, and re-layouts  1.38 us (2%)
  between operations  1.3 us (2%)
    pallas_call x1, Pallas kernels, body(): pl.pallas_call(functools.partial(kernel, along_z, bins), out_shape=jax.Sh...  78.7 us

profile of v4, /device:TPU:1, one launch (start us, length us, event | category | flops | bytes accessed | tf_op | source)
XLA Modules:
  0.0 81.4 jit_solution(2868281784365331626)
XLA Ops:
  1.3 78.7 %shard_map.73 = f32[4,4,512]{2,1,0:T(4,128)} custom-call(bf16[8,4,256,256]{3,2,1,0:T(8,128)(2,1)} %tiles_hbm.1, s32[2,8]{1,0:T(2,128)} %pattern_hbm.1, s32[1]{0:T(128)S(6)} %copy.9.count, f32[4,4,512]{2,1,0:T(4,128)} %map_hbm.1, f32[4,4,128]{2,1,0:T(4,128)} %measured_hbm.1, f32[1]{0:T(128)S(6)} %copy.10.step_ref, f32[1,512]{1,0:T(1,128)} %bitcast.1), custom_call_target="tpu_custom_call" | custom-call | tf_op jit(solution)/shard_map/pallas_call | solution.py:273
  80.0 1.4 %copy.11 = f32[4,4,512]{2,1,0:T(4,128)} copy(f32[4,4,512]{2,1,0:T(4,128)} %shard_map.73) | data formatting | bytes 65536

commit v5 on v4

--- a/solution.py
+++ b/solution.py
@@ -15,8 +15,8 @@
 BATCHES = 1
 
 
-def kernel(along_z, bins, tiles_hbm, pattern_hbm, count, map_hbm, measured_hbm, step_ref, penalty_hbm, out_ref,
-           pattern, map_ref, measured_ref, penalty_ref, tiles, turned, current, sources, measured, lookup_out, lookup_in, lookup_smem, sums_matrix,
+def kernel(along_z, bins, tiles_hbm, pattern_hbm, count_hbm, map_hbm, measured_hbm, step_hbm, penalty_hbm, out_ref,
+           pattern, count, map_ref, measured_ref, step_ref, penalty_ref, tiles, turned, current, sources, measured, lookup_out, lookup_in, lookup_smem, sums_matrix,
            part_out, part_in, pieces, chunk_out, chunk_in, rounded_in, gather_out, gather_in, energy_out, energy_in,
            tile_sem, input_sem, smem_sem, send_sem, recv_sem):
     slots, bins_dev, tile, _ = tiles.shape
@@ -54,7 +54,8 @@
         pl.semaphore_signal(barrier, inc=1, device_id=peer, device_id_type=MESH)
     inputs = []
     for i, (there, here) in enumerate((
-        (pattern_hbm, pattern), (map_hbm, map_ref), (measured_hbm, measured_ref), (penalty_hbm, penalty_ref),
+        (map_hbm, map_ref), (pattern_hbm, pattern), (count_hbm, count), (measured_hbm, measured_ref), (step_hbm, step_ref),
+        (penalty_hbm, penalty_ref),
     )):
         load = pltpu.make_async_copy(there, here, input_sem.at[i])
         load.start()
@@ -90,14 +91,12 @@
 
     lane_slot = lax.broadcasted_iota(jnp.int32, (8, 128), 1) // rows
     names = jnp.zeros((8, 128), jnp.int32)
-    live = jnp.zeros((8, 128), jnp.int32)
     for s in range(slots):
         names = jnp.where(lane_slot == s, pattern[0, s], names)
-        live = jnp.where(lane_slot == s, (s < count[0]).astype(jnp.int32), live)
     place = lax.rem(z + along_z - names // ALONG_X, along_z)
     for dx in range(ALONG_X):
         there = lax.rem(x + dx, ALONG_X)
-        wanted = jnp.where((lax.rem(names, ALONG_X) == there) & (live == 1), place, along_z)
+        wanted = jnp.where((lax.rem(names, ALONG_X) == there) & (lane_slot < count[...]), place, along_z)
         lookup_out[dx] = wanted
         if dx == 0:
             lookup_in[0] = wanted
@@ -108,7 +107,7 @@
         for t in range(2):
             current[t, at, :] = map_ref[f, :, pl.ds(t * tile, tile)]
     row_bin = lax.broadcasted_iota(jnp.int32, (rows, tile), 0) // snaps
-    step_size = step_ref[0]
+    step_size = step_ref[...]
     zeros = jnp.zeros((rows, half), jnp.bfloat16)
     lane = lax.broadcasted_iota(jnp.int32, (rows, 128), 1)
 
@@ -269,16 +268,18 @@
         points, few = initial_map.shape[2], slots // BATCHES
         bf16, f32 = jnp.bfloat16, jnp.float32
         exchanges = 1 + ((ALONG_X + 1) * BATCHES + 3) * ITERS
-        hbm, smem = pl.BlockSpec(memory_space=pltpu.HBM), pl.BlockSpec(memory_space=pltpu.SMEM)
+        hbm = pl.BlockSpec(memory_space=pltpu.HBM)
         return pl.pallas_call(
             functools.partial(kernel, along_z, bins),
             out_shape=jax.ShapeDtypeStruct(initial_map.shape, f32),
-            in_specs=[hbm, hbm, smem, hbm, hbm, smem, hbm],
+            in_specs=[hbm] * 7,
             out_specs=pl.BlockSpec(memory_space=pltpu.VMEM),
             scratch_shapes=[
                 pltpu.SMEM(tile_pattern.shape, jnp.int32),
+                pltpu.VMEM((1, 1), jnp.int32),
                 pltpu.VMEM(initial_map.shape, f32),
                 pltpu.VMEM(measured.shape, f32),
+                pltpu.VMEM((1, 1), f32),
                 pltpu.VMEM((1, points), f32),
                 pltpu.VMEM((slots, bins_dev, tile, tile), bf16),
                 pltpu.VMEM((slots, bins_dev * tile, tile), bf16),
@@ -300,7 +301,7 @@
                 pltpu.VMEM((ITERS, 1, points), f32),
                 pltpu.VMEM((ITERS, bins, 1, points), f32),
                 pltpu.SemaphoreType.DMA((slots,)),
-                pltpu.SemaphoreType.DMA((4,)),
+                pltpu.SemaphoreType.DMA((6,)),
                 pltpu.SemaphoreType.DMA((1,)),
                 pltpu.SemaphoreType.DMA((exchanges,)),
                 pltpu.SemaphoreType.DMA((exchanges,)),
@@ -308,7 +309,10 @@
             compiler_params=pltpu.CompilerParams(
                 collective_id=0, has_side_effects=True, vmem_limit_bytes=56 * 1024 * 1024
             ),
-        )(tile_blocks, tile_pattern, tile_count, initial_map, measured, step_size, penalty.reshape(1, points))
+        )(
+            tile_blocks, tile_pattern, tile_count.reshape(1, 1), initial_map, measured, step_size.reshape(1, 1),
+            penalty.reshape(1, points),
+        )
 
     in_specs = (
         P("scan", "bin", None, None),

time: 81.6 us -> 81.4 us (level)
  no operation moved by 1% of the time
where the time goes in v5:
time: 81.4 us; the launch traced here: 81.2 us
  Pallas kernels  78.5 us (96%)
  local copies, waits for them, and re-layouts  1.38 us (2%)
  between operations  1.3 us (2%)
    pallas_call x1, Pallas kernels, body(): pl.pallas_call(functools.partial(kernel, along_z, bins), out_shape=jax.Sh...  78.5 us

profile of v5, /device:TPU:1, one launch (start us, length us, event | category | flops | bytes accessed | tf_op | source)
XLA Modules:
  0.0 81.2 jit_solution(5480447268379487830)
XLA Ops:
  1.3 78.5 %shard_map.73 = f32[4,4,512]{2,1,0:T(4,128)} custom-call(bf16[8,4,256,256]{3,2,1,0:T(8,128)(2,1)} %tiles_hbm.1, s32[2,8]{1,0:T(2,128)} %pattern_hbm.1, s32[1,1]{1,0:T(1,128)} %bitcast.3.count_hbm, f32[4,4,512]{2,1,0:T(4,128)} %map_hbm.1, f32[4,4,128]{2,1,0:T(4,128)} %measured_hbm.1, f32[1,1]{1,0:T(1,128)} %bitcast.4.step_hbm, f32[1,512]{1,0:T(1,128)} %bitcast.5), custom_call_target="tpu_custom_call" | custom-call | tf_op jit(solution)/shard_map/pallas_call | solution.py:272
  79.8 1.4 %copy.11 = f32[4,4,512]{2,1,0:T(4,128)} copy(f32[4,4,512]{2,1,0:T(4,128)} %shard_map.73) | data formatting | bytes 65536

commit v6 on v5

--- a/solution.py
+++ b/solution.py
@@ -15,8 +15,8 @@
 BATCHES = 1
 
 
-def kernel(along_z, bins, tiles_hbm, pattern_hbm, count_hbm, map_hbm, measured_hbm, step_hbm, penalty_hbm, out_ref,
-           pattern, count, map_ref, measured_ref, step_ref, penalty_ref, tiles, turned, current, sources, measured, lookup_out, lookup_in, lookup_smem, sums_matrix,
+def kernel(along_z, bins, tiles_hbm, pattern, count_hbm, map_hbm, measured_hbm, step_hbm, penalty_hbm, out_ref,
+           count, map_ref, measured_ref, step_ref, penalty_ref, tiles, turned, current, sources, measured, lookup_out, lookup_in, lookup_smem, sums_matrix,
            part_out, part_in, pieces, chunk_out, chunk_in, rounded_in, gather_out, gather_in, energy_out, energy_in,
            tile_sem, input_sem, smem_sem, send_sem, recv_sem):
     slots, bins_dev, tile, _ = tiles.shape
@@ -54,7 +54,7 @@
         pl.semaphore_signal(barrier, inc=1, device_id=peer, device_id_type=MESH)
     inputs = []
     for i, (there, here) in enumerate((
-        (map_hbm, map_ref), (pattern_hbm, pattern), (count_hbm, count), (measured_hbm, measured_ref), (step_hbm, step_ref),
+        (map_hbm, map_ref), (count_hbm, count), (measured_hbm, measured_ref), (step_hbm, step_ref),
         (penalty_hbm, penalty_ref),
     )):
         load = pltpu.make_async_copy(there, here, input_sem.at[i])
@@ -272,10 +272,9 @@
         return pl.pallas_call(
             functools.partial(kernel, along_z, bins),
             out_shape=jax.ShapeDtypeStruct(initial_map.shape, f32),
-            in_specs=[hbm] * 7,
+            in_specs=[hbm, pl.BlockSpec(memory_space=pltpu.SMEM)] + [hbm] * 5,
             out_specs=pl.BlockSpec(memory_space=pltpu.VMEM),
             scratch_shapes=[
-                pltpu.SMEM(tile_pattern.shape, jnp.int32),
                 pltpu.VMEM((1, 1), jnp.int32),
                 pltpu.VMEM(initial_map.shape, f32),
                 pltpu.VMEM(measured.shape, f32),
@@ -301,13 +300,13 @@
                 pltpu.VMEM((ITERS, 1, points), f32),
                 pltpu.VMEM((ITERS, bins, 1, points), f32),
                 pltpu.SemaphoreType.DMA((slots,)),
-                pltpu.SemaphoreType.DMA((6,)),
+                pltpu.SemaphoreType.DMA((5,)),
                 pltpu.SemaphoreType.DMA((1,)),
                 pltpu.SemaphoreType.DMA((exchanges,)),
                 pltpu.SemaphoreType.DMA((exchanges,)),
             ],
             compiler_params=pltpu.CompilerParams(
-                collective_id=0, has_side_effects=True, vmem_limit_bytes=56 * 1024 * 1024
+                collective_id=0, has_side_effects=True, vmem_limit_bytes=55168 * 1024
             ),
         )(
             tile_blocks, tile_pattern, tile_count.reshape(1, 1), initial_map, measured, step_size.reshape(1, 1),

time: 81.4 us -> 82.2 us (level)
  local copies, waits for them, and re-layouts: 1.38 us -> 2.67 us
    unnamed x1 -> x7, local copies, waits for them, and re-layouts: 1.38 us -> 2.67 us
where the time goes in v6:
time: 82.2 us; the launch traced here: 82 us
  Pallas kernels  78 us (95%)
  local copies, waits for them, and re-layouts  2.67 us (3%)
  between operations  1.32 us (2%)
    pallas_call x1, Pallas kernels, body(): pl.pallas_call(functools.partial(kernel, along_z, bins), out_shape=jax.Sh...  78 us
    unnamed x7, local copies, waits for them, and re-layouts  2.67 us

profile of v6, /device:TPU:1, one launch (start us, length us, event | category | flops | bytes accessed | tf_op | source)
XLA Modules:
  0.0 82.0 jit_solution(5910024653643636794)
XLA Ops:
  1.3 0.0 copy-start
  1.3 0.7 copy-done
  2.0 0.0 copy-start.1
  2.0 0.7 copy-done.1
  2.7 0.0 copy-start.2
  2.7 0.7 copy-done.2
  3.4 78.0 %shard_map.73 = f32[4,4,512]{2,1,0:T(4,128)S(1)} custom-call(bf16[8,4,256,256]{3,2,1,0:T(8,128)(2,1)} %tiles_hbm.1, s32[2,8]{1,0:T(2,128)S(1)} %copy-done.2, s32[1,1]{1,0:T(1,128)} %bitcast.3.count_hbm, f32[4,4,512]{2,1,0:T(4,128)} %map_hbm.1, f32[4,4,128]{2,1,0:T(4,128)S(1)} %copy-done, f32[1,1]{1,0:T(1,128)} %bitcast.4.step_hbm, f32[1,512]{1,0:T(1,128)S(1)} %bitcast.5), custom_call_target="tpu_custom_call" | custom-call | tf_op jit(solution)/shard_map/pallas_call | solution.py:272
  81.4 0.6 copy.11
Async XLA Ops:
  1.3 0.7 copy-start
  2.0 0.7 copy-start.1
  2.7 0.7 copy-start.2
